TPU v7x, 32 devices: a whole 2x2x4 slice. The times are simulated.
32 devices in a mesh: req: 16 (over z, x, core), tp: 2 (over y).
Axes of the slice: x: 2, y: 2, z: 4, core: 2. Of those that a mesh axis runs over, the one named last changes fastest.
Arguments:
- q_new: bfloat16 [1024, 5120], P('req', 'tp'), may hold values from -6 to 6
- k_new: bfloat16 [1024, 1024], P('req', 'tp'), may hold values from -15 to 15
- v_new: bfloat16 [1024, 1024], P('req', 'tp'), may hold values from -6 to 6
- k_cache: bfloat16 [256, 128, 1024], P('req', None, 'tp'), may hold values from -16 to 16
- v_cache: bfloat16 [256, 128, 1024], P('req', None, 'tp'), may hold values from -6 to 6
- lengths: int32 [8], replicated, may hold values from 1 to 4096, as said below
- page_table: int32 [8, 32], replicated, may hold values from -1 to 255, as said below
- w_out: bfloat16 [5120, 5120], P('req', 'tp'), may hold values from -0.078125 to 0.078125
Outputs:
- attn_out: bfloat16 [1024, 5120], P('req')
Inputs may be any that keep to these rules, and one draw needn't show every extreme that they name: `lengths`: the last request, 7, has exactly 4096 cached tokens; every request has at least one. `page_table`: request r uses ceil(lengths[r] / 128) logical pages. Its first ceil(ceil(lengths[r] / 128) / 2) logical pages lie among global pages 2r * 16 to (2r + 1) * 16 - 1, the rest among (2r + 1) * 16 to (2r + 2) * 16 - 1; distinct logical pages use distinct global pages; entries past a request's last page are -1.
All inputs are finite; a program needn't handle non-finite values.
Results may differ from a plain program's by a relative error of at most 0.024.
Values may be sent and summed in bfloat16 or wider, within the bound.
A program may use at most 128 MiB of HBM per device.

v0:
```python
import math

import jax
import jax.numpy as jnp
from jax import lax
from jax.sharding import PartitionSpec as P

HD = 128
GROUP = 5
BLOCK_PAGES = 4


ROPE_BASE = 1000000.0
FLOOR_SCORE = -1e30


def from_partner(value, axis, distance):
    return lax.ppermute(value, axis, [(i, i ^ 1 << distance) for i in range(lax.axis_size(axis))])


def rotate(values, places):
    inverse = 1.0 / ROPE_BASE ** (jnp.arange(0, HD, 2).astype(jnp.float32) / HD)
    angles = places.astype(jnp.float32)[:, None] * inverse[None, :]
    cosine = jnp.concatenate([jnp.cos(angles), jnp.cos(angles)], axis=-1)[:, None, :]
    sine = jnp.concatenate([jnp.sin(angles), jnp.sin(angles)], axis=-1)[:, None, :]
    first_half = values[..., : HD // 2]
    second_half = values[..., HD // 2 :]
    turned = jnp.concatenate([-second_half, first_half], axis=-1)
    return values * cosine + turned * sine


def absorb(state, queries, block_keys, block_values, allowed, scale):
    running_max, running_sum, output = state
    scores = (
        jnp.einsum("qcgd,kcd->cgqk", queries, block_keys, preferred_element_type=jnp.float32)
        * scale
    )
    scores = jnp.where(allowed[None, None], scores, FLOOR_SCORE)
    new_max = jnp.maximum(running_max, jnp.max(scores, axis=-1))
    factor = jnp.exp(running_max - new_max)
    weights = jnp.where(allowed[None, None], jnp.exp(scores - new_max[..., None]), 0.0)
    running_sum = running_sum * factor + jnp.sum(weights, axis=-1)
    mixed = jnp.einsum(
        "cgqk,kcd->qcgd",
        weights.astype(jnp.bfloat16),
        block_values,
        preferred_element_type=jnp.float32,
    )
    output = output * jnp.transpose(factor, (2, 0, 1))[..., None] + mixed
    return (new_max, running_sum, output)


def tensor_total(partial_value):
    return lax.psum(partial_value.astype(jnp.bfloat16), "tp")


def shards(q_new, k_new, v_new, k_cache, v_cache, lengths, page_table, w_out):
    own_rows = q_new.shape[0]
    all_rows = 2 * own_rows
    local_heads = k_new.shape[1] // HD
    pages_local = k_cache.shape[0]
    page_rows = k_cache.shape[1]
    block_rows = BLOCK_PAGES * page_rows
    scale = 1.0 / math.sqrt(HD)
    device_row = lax.axis_index("req")
    parity = device_row % 2
    request = device_row // 2
    length = lengths[request]
    own_places = length + parity * own_rows + jnp.arange(own_rows)
    own_queries = rotate(
        q_new.reshape(own_rows, local_heads * GROUP, HD).astype(jnp.float32), own_places
    ).astype(jnp.bfloat16)
    own_keys = rotate(
        k_new.reshape(own_rows, local_heads, HD).astype(jnp.float32), own_places
    ).astype(jnp.bfloat16)
    own_values = v_new.reshape(own_rows, local_heads, HD)
    peer_queries, peer_keys, peer_values = from_partner(
        (own_queries, own_keys, own_values), "req", 0
    )

    def ordered(mine, theirs):
        return jnp.where(
            parity == 0,
            jnp.concatenate([mine, theirs], axis=0),
            jnp.concatenate([theirs, mine], axis=0),
        )

    queries = ordered(own_queries, peer_queries).reshape(all_rows, local_heads, GROUP, HD)
    fresh_keys = ordered(own_keys, peer_keys)
    fresh_values = ordered(own_values, peer_values)
    state = (
        jnp.full((local_heads, GROUP, all_rows), FLOOR_SCORE, jnp.float32),
        jnp.zeros((local_heads, GROUP, all_rows), jnp.float32),
        jnp.zeros((all_rows, local_heads, GROUP, HD), jnp.float32),
    )
    token_index = jnp.arange(all_rows)
    causal = (token_index[None, :] <= token_index[:, None]) & (parity == 1)
    state = absorb(state, queries, fresh_keys, fresh_values, causal, scale)
    page_count = (length + page_rows - 1) // page_rows
    even_pages = (page_count + 1) // 2
    first_page = jnp.where(parity == 0, 0, even_pages)
    last_page = jnp.where(parity == 0, even_pages, page_count)
    table_row = jnp.concatenate([page_table[request], jnp.full((BLOCK_PAGES,), -1, jnp.int32)])
    offset = device_row * pages_local
    block_count = (last_page - first_page + BLOCK_PAGES - 1) // BLOCK_PAGES

    def visit(block, carry):
        block_first = first_page + block * BLOCK_PAGES
        logical = block_first + jnp.arange(BLOCK_PAGES)
        physical = lax.dynamic_slice(table_row, (block_first,), (BLOCK_PAGES,))
        slots = jnp.clip(physical - offset, 0, pages_local - 1)
        block_keys = k_cache[slots].reshape(block_rows, local_heads, HD)
        block_values = v_cache[slots].reshape(block_rows, local_heads, HD)
        key_places = (logical[:, None] * page_rows + jnp.arange(page_rows)[None, :]).reshape(
            block_rows
        )
        usable = jnp.repeat(logical < last_page, page_rows) & (key_places < length)
        allowed = jnp.broadcast_to(usable[None, :], (all_rows, block_rows))
        return absorb(carry, queries, block_keys, block_values, allowed, scale)

    running_max, running_sum, output = lax.fori_loop(0, block_count, visit, state)
    peer_start = (1 - parity) * own_rows
    own_start = parity * own_rows
    outgoing = (
        lax.dynamic_slice_in_dim(output, peer_start, own_rows, 0),
        lax.dynamic_slice_in_dim(running_max, peer_start, own_rows, 2),
        lax.dynamic_slice_in_dim(running_sum, peer_start, own_rows, 2),
    )
    other_output, other_max, other_sum = (
        from_partner(outgoing[0].astype(jnp.bfloat16), "req", 0).astype(jnp.float32),
        from_partner(outgoing[1].astype(jnp.bfloat16), "req", 0).astype(jnp.float32),
        from_partner(outgoing[2].astype(jnp.bfloat16), "req", 0).astype(jnp.float32),
    )
    mine_output = lax.dynamic_slice_in_dim(output, own_start, own_rows, 0)
    mine_max = lax.dynamic_slice_in_dim(running_max, own_start, own_rows, 2)
    mine_sum = lax.dynamic_slice_in_dim(running_sum, own_start, own_rows, 2)
    joint_max = jnp.maximum(mine_max, other_max)
    mine_factor = jnp.exp(mine_max - joint_max)
    other_factor = jnp.exp(other_max - joint_max)
    joint_sum = mine_sum * mine_factor + other_sum * other_factor
    joint_output = (
        mine_output * jnp.transpose(mine_factor, (2, 0, 1))[..., None]
        + other_output * jnp.transpose(other_factor, (2, 0, 1))[..., None]
    )
    attention = (
        (joint_output / jnp.transpose(joint_sum, (2, 0, 1))[..., None])
        .reshape(own_rows, local_heads * GROUP * HD)
        .astype(jnp.bfloat16)
    )
    partial_value = lax.dot_general(
        attention,
        lax.all_gather(w_out, "req", axis=0, tiled=True),
        (((1,), (1,)), ((), ())),
        preferred_element_type=jnp.float32,
    )
    return tensor_total(partial_value)


def solution(mesh):
    in_specs = (
        P("req", "tp"),
        P("req", "tp"),
        P("req", "tp"),
        P("req", None, "tp"),
        P("req", None, "tp"),
        P(),
        P(),
        P("req", "tp"),
    )
    out_specs = P("req", None)
    return jax.shard_map(shards, mesh=mesh, in_specs=in_specs, out_specs=out_specs, check_vma=False)
```

profile of v0, /device:TPU:0, one launch (start us, length us, event | category | flops | bytes accessed | tf_op | source)
XLA Modules:
  0.0 199.3 jit_solution(11748223792716018775)
XLA Ops:
  6.5 0.7 all-gather.2.cloned.1.call-update
  7.7 0.6 dynamic_slice.27
  9.5 1.1 fusion.33
  10.5 0.5 collective-permute-start.1
  11.3 0.7 fusion.39
  12.2 0.5 collective-permute-start.2
  13.5 1.0 copy.95
  14.9 0.4 copy.96
  15.3 0.7 copy-done.1
  15.9 0.4 copy.97
  16.4 0.4 fusion.31
  16.9 1.1 copy.98
  18.2 0.4 maximum_select_fusion
  19.0 1.8 fusion.67
  21.1 2.6 %fusion.27 = f32[128,4,5,128]{0,3,2,1:T(8,128)} fusion(f32[4,5,128,128]{2,3,1,0:T(8,128)S(1)} %get-tuple-element.172, f32[128,4,5]{0,2,1:T(8,128)S(1)} %get-tuple-element.167, f32[4,5,128]{2,1,0:T(8,128)S(1)} %broadcast_maximum_fusion, pred[128,128]{0,1:T(8,128)(4,1)S(1)} %fusion.56, bf16[64,4,128]{0,2,1:T(8,128)(2,1)} %collective-permute-done.2, ...), kind=kOutput, calls=%fused_computation.36 | convolution fusion | flops 85786624 | bytes 2789377 | tf_op jit(solution)/shard_map/cgqk,kcd->qcgd/dot_general | solution.py:43
  23.6 65.6 %while.14 = (s32[]{:T(128)}, f32[4,5,128]{2,1,0:T(8,128)S(1)}, f32[4,5,128]{2,1,0:T(8,128)S(1)}, f32[128,4,5,128]{0,3,2,1:T(8,128)}, s32[]{:T(128)}, /*index=5*/...) while((s32[]{:T(128)}, f32[4,5,128]{2,1,0:T(8,128)S(1)}, ...), condition=%wide.region_5.6_spmd, body=%wide.region_2.5_spmd.sunk | while | flops 688793600 | bytes 40147352 | solution.py:121
  23.7 2.2 %gather_fusion = bf16[4,128,512]{2,1,0:T(8,128)(2,1)S(1)} fusion(bf16[16,128,512]{2,1,0:T(8,128)(2,1)} %get-tuple-element.307, s32[1024]{0:T(1024)S(1)} %pad_clamp_fusion.2), kind=kCustom, calls=%fused_computation.clone.1 | custom fusion | bytes 1048592 | tf_op jit(solution)/shard_map/while/body/gather | solution.py:112
  26.1 0.6 fusion.86
  26.7 3.3 %bitcast_reduce_fusion.2 = (f32[4,5,128]{2,1,0:T(8,128)S(1)}, f32[4,512,128,5]{2,1,3,0:T(8,128)}) fusion(pred[512]{0:T(512)(128)(4,1)S(1)} %fusion.86, bf16[128,4,5,128]{3,0,2,1:T(8,128)(2,1)S(1)} %get-tuple-element.308, bf16[512,4,128,1]{2,1,0,3:T(4,128)(2,1)S(1)} %bitcast.86), kind=kOutput, calls=%fused_computation.3.clone.1 | convolution fusion | flops 339473920 | bytes 6433280 | tf_op jit(solution)/shard_map/while/body/qcgd,kcd->cgqk/dot_general | solution.py:35
  30.0 2.2 %gather_fusion.1 = bf16[4,128,512]{2,1,0:T(8,128)(2,1)S(1)} fusion(bf16[16,128,512]{2,1,0:T(8,128)(2,1)} %get-tuple-element.309, s32[1024]{0:T(1024)S(1)} %pad_clamp_fusion.2), kind=kCustom, calls=%fused_computation.1.clone.1 | custom fusion | bytes 1048592 | tf_op jit(solution)/shard_map/while/body/gather | solution.py:113
  32.4 5.9 %fusion.89 = f32[128,4,5,128]{0,3,2,1:T(8,128)} fusion(f32[4,512,128,5]{2,1,3,0:T(8,128)} %get-tuple-element.261, f32[4,5,128]{2,1,0:T(8,128)S(1)} %get-tuple-element.298, pred[512]{0:T(512)(128)(4,1)S(1)} %fusion.86, f32[128,4,5,128]{0,3,2,1:T(8,128)} %get-tuple-element.283, f32[128,4,5]{0,2,1:T(8,128)S(1)} %get-tuple-element.262, ...), kind=kOutput, calls=%fused_computation.13.clone.1 | convolution fusion | flops 342753280 | bytes 8409600 | tf_op jit(solution)/shard_map/while/body/cgqk,kcd->qcgd/dot_general | solution.py:43
  38.3 1.7 fusion.88
  40.1 2.2 %gather_fusion = bf16[4,128,512]{2,1,0:T(8,128)(2,1)S(1)} fusion(bf16[16,128,512]{2,1,0:T(8,128)(2,1)} %get-tuple-element.307, s32[1024]{0:T(1024)S(1)} %pad_clamp_fusion.2), kind=kCustom, calls=%fused_computation.clone.1 | custom fusion | bytes 1048592 | tf_op jit(solution)/shard_map/while/body/gather | solution.py:112
  42.5 0.6 fusion.86
  43.1 3.3 %bitcast_reduce_fusion.2 = (f32[4,5,128]{2,1,0:T(8,128)S(1)}, f32[4,512,128,5]{2,1,3,0:T(8,128)}) fusion(pred[512]{0:T(512)(128)(4,1)S(1)} %fusion.86, bf16[128,4,5,128]{3,0,2,1:T(8,128)(2,1)S(1)} %get-tuple-element.308, bf16[512,4,128,1]{2,1,0,3:T(4,128)(2,1)S(1)} %bitcast.86), kind=kOutput, calls=%fused_computation.3.clone.1 | convolution fusion | flops 339473920 | bytes 6433280 | tf_op jit(solution)/shard_map/while/body/qcgd,kcd->cgqk/dot_general | solution.py:35
  46.5 2.2 %gather_fusion.1 = bf16[4,128,512]{2,1,0:T(8,128)(2,1)S(1)} fusion(bf16[16,128,512]{2,1,0:T(8,128)(2,1)} %get-tuple-element.309, s32[1024]{0:T(1024)S(1)} %pad_clamp_fusion.2), kind=kCustom, calls=%fused_computation.1.clone.1 | custom fusion | bytes 1048592 | tf_op jit(solution)/shard_map/while/body/gather | solution.py:113
  48.8 5.7 %fusion.89 = f32[128,4,5,128]{0,3,2,1:T(8,128)} fusion(f32[4,512,128,5]{2,1,3,0:T(8,128)} %get-tuple-element.261, f32[4,5,128]{2,1,0:T(8,128)S(1)} %get-tuple-element.298, pred[512]{0:T(512)(128)(4,1)S(1)} %fusion.86, f32[128,4,5,128]{0,3,2,1:T(8,128)} %get-tuple-element.283, f32[128,4,5]{0,2,1:T(8,128)S(1)} %get-tuple-element.262, ...), kind=kOutput, calls=%fused_computation.13.clone.1 | convolution fusion | flops 342753280 | bytes 8409600 | tf_op jit(solution)/shard_map/while/body/cgqk,kcd->qcgd/dot_general | solution.py:43
  54.5 1.7 fusion.88
  56.4 2.2 %gather_fusion = bf16[4,128,512]{2,1,0:T(8,128)(2,1)S(1)} fusion(bf16[16,128,512]{2,1,0:T(8,128)(2,1)} %get-tuple-element.307, s32[1024]{0:T(1024)S(1)} %pad_clamp_fusion.2), kind=kCustom, calls=%fused_computation.clone.1 | custom fusion | bytes 1048592 | tf_op jit(solution)/shard_map/while/body/gather | solution.py:112
  58.7 0.6 fusion.86
  59.4 3.3 %bitcast_reduce_fusion.2 = (f32[4,5,128]{2,1,0:T(8,128)S(1)}, f32[4,512,128,5]{2,1,3,0:T(8,128)}) fusion(pred[512]{0:T(512)(128)(4,1)S(1)} %fusion.86, bf16[128,4,5,128]{3,0,2,1:T(8,128)(2,1)S(1)} %get-tuple-element.308, bf16[512,4,128,1]{2,1,0,3:T(4,128)(2,1)S(1)} %bitcast.86), kind=kOutput, calls=%fused_computation.3.clone.1 | convolution fusion | flops 339473920 | bytes 6433280 | tf_op jit(solution)/shard_map/while/body/qcgd,kcd->cgqk/dot_general | solution.py:35
  62.7 2.2 %gather_fusion.1 = bf16[4,128,512]{2,1,0:T(8,128)(2,1)S(1)} fusion(bf16[16,128,512]{2,1,0:T(8,128)(2,1)} %get-tuple-element.309, s32[1024]{0:T(1024)S(1)} %pad_clamp_fusion.2), kind=kCustom, calls=%fused_computation.1.clone.1 | custom fusion | bytes 1048592 | tf_op jit(solution)/shard_map/while/body/gather | solution.py:113
  65.1 5.8 %fusion.89 = f32[128,4,5,128]{0,3,2,1:T(8,128)} fusion(f32[4,512,128,5]{2,1,3,0:T(8,128)} %get-tuple-element.261, f32[4,5,128]{2,1,0:T(8,128)S(1)} %get-tuple-element.298, pred[512]{0:T(512)(128)(4,1)S(1)} %fusion.86, f32[128,4,5,128]{0,3,2,1:T(8,128)} %get-tuple-element.283, f32[128,4,5]{0,2,1:T(8,128)S(1)} %get-tuple-element.262, ...), kind=kOutput, calls=%fused_computation.13.clone.1 | convolution fusion | flops 342753280 | bytes 8409600 | tf_op jit(solution)/shard_map/while/body/cgqk,kcd->qcgd/dot_general | solution.py:43
  70.9 1.7 fusion.88
  72.7 2.2 %gather_fusion = bf16[4,128,512]{2,1,0:T(8,128)(2,1)S(1)} fusion(bf16[16,128,512]{2,1,0:T(8,128)(2,1)} %get-tuple-element.307, s32[1024]{0:T(1024)S(1)} %pad_clamp_fusion.2), kind=kCustom, calls=%fused_computation.clone.1 | custom fusion | bytes 1048592 | tf_op jit(solution)/shard_map/while/body/gather | solution.py:112
  75.1 0.6 fusion.86
  75.7 3.3 %bitcast_reduce_fusion.2 = (f32[4,5,128]{2,1,0:T(8,128)S(1)}, f32[4,512,128,5]{2,1,3,0:T(8,128)}) fusion(pred[512]{0:T(512)(128)(4,1)S(1)} %fusion.86, bf16[128,4,5,128]{3,0,2,1:T(8,128)(2,1)S(1)} %get-tuple-element.308, bf16[512,4,128,1]{2,1,0,3:T(4,128)(2,1)S(1)} %bitcast.86), kind=kOutput, calls=%fused_computation.3.clone.1 | convolution fusion | flops 339473920 | bytes 6433280 | tf_op jit(solution)/shard_map/while/body/qcgd,kcd->cgqk/dot_general | solution.py:35
  79.0 2.2 %gather_fusion.1 = bf16[4,128,512]{2,1,0:T(8,128)(2,1)S(1)} fusion(bf16[16,128,512]{2,1,0:T(8,128)(2,1)} %get-tuple-element.309, s32[1024]{0:T(1024)S(1)} %pad_clamp_fusion.2), kind=kCustom, calls=%fused_computation.1.clone.1 | custom fusion | bytes 1048592 | tf_op jit(solution)/shard_map/while/body/gather | solution.py:113
  81.4 5.9 %fusion.89 = f32[128,4,5,128]{0,3,2,1:T(8,128)} fusion(f32[4,512,128,5]{2,1,3,0:T(8,128)} %get-tuple-element.261, f32[4,5,128]{2,1,0:T(8,128)S(1)} %get-tuple-element.298, pred[512]{0:T(512)(128)(4,1)S(1)} %fusion.86, f32[128,4,5,128]{0,3,2,1:T(8,128)} %get-tuple-element.283, f32[128,4,5]{0,2,1:T(8,128)S(1)} %get-tuple-element.262, ...), kind=kOutput, calls=%fused_computation.13.clone.1 | convolution fusion | flops 342753280 | bytes 8409600 | tf_op jit(solution)/shard_map/while/body/cgqk,kcd->qcgd/dot_general | solution.py:43
  87.3 1.7 fusion.88
  89.7 1.7 copy.108
  92.1 1.0 collective-permute-done.5
  93.2 0.6 divide_convert_fusion
  94.1 0.4 convert_element_type.95
  94.5 50.8 %all-gather.2.cloned.1.call-done = bf16[5120,2560]{1,0:T(8,128)(2,1)} async-done(((bf16[320,2560]{1,0:T(8,128)(2,1)}), bf16[5120,2560]{1,0:T(8,128)(2,1)}) %all-gather.2.cloned.1.call-update) | async-done | bytes 26214416 | tf_op jit(solution)/shard_map/all_gather | solution.py:152
  145.2 13.7 %convolution_convert_fusion = bf16[64,5120]{1,0:T(8,128)(2,1)} fusion(bf16[64,2560]{1,0:T(8,128)(2,1)S(1)} %convert_element_type.95, bf16[5120,2560]{1,0:T(8,128)(2,1)} %all-gather.2.cloned.1.call-done), kind=kOutput, calls=%fused_computation.31 | convolution fusion | flops 1678049280 | bytes 27197440 | tf_op jit(solution)/shard_map/dot_general | solution.py:150
  158.9 31.6 %all-reduce.3.cloned.1.call-done = bf16[64,5120]{1,0:T(8,128)(2,1)} async-done(((bf16[64,5120]{1,0:T(8,128)(2,1)}), bf16[64,5120]{1,0:T(8,128)(2,1)}) %all-reduce.3.cloned.1.call-update) | async-done | bytes 655376 | tf_op jit(solution)/shard_map/psum | solution.py:54
  190.5 2.0 copy.148
  (105 shorter events, 5.8 us)
Async XLA Ops:
  6.5 9.8 %copy-start = (s32[8,32]{1,0:T(8,128)S(1)}, s32[8,32]{1,0:T(8,128)}, u32[]{:S(2)}) copy-start(s32[8,32]{1,0:T(8,128)} %param.16) | copy-start | bytes 3076
  6.5 1.0 copy-start.2
  6.5 1.2 copy-start.5
  6.5 138.7 %all-gather.2.cloned.1.call-start = ((), (), s32[]{:S(2)}) async-start(), calls=%async_computation | async-start | bytes 27852800 | tf_op jit(solution)/shard_map/all_gather | solution.py:152
  7.3 183.3 %all-reduce.3.cloned.1.call-start = ((), (), s32[]{:S(2)}) async-start(), calls=%async_computation.1 | async-start | bytes 1310720 | tf_op jit(solution)/shard_map/psum | solution.py:54
  9.5 1.7 copy-start.3
  10.5 1.6 copy-start.4
  10.5 6.3 %collective-permute-start.1 = (bf16[64,20,128]{2,1,0:T(8,128)(2,1)}, bf16[64,20,128]{2,1,0:T(8,128)(2,1)}, u32[]{:S(2)}, u32[]{:S(2)}) collective-permute-start(bf16[64,20,128]{2,1,0:T(8,128)(2,1)} %fusion.33), channel_id=1, source_target_pairs={{0,2},{2,0},{4,6},{6,4},{8,10},{10,8},{12,14},{14,12},{16,18},{18,... | collective-permute-start | bytes 983048 | tf_op jit(solution)/shard_map/ppermute | solution.py:18
  12.0 6.9 %collective-permute-start = (bf16[64,4,128]{0,2,1:T(8,128)(2,1)}, bf16[64,4,128]{0,2,1:T(8,128)(2,1)}, u32[]{:S(2)}, u32[]{:S(2)}) collective-permute-start(bf16[64,4,128]{0,2,1:T(8,128)(2,1)} %fusion.39), channel_id=1, source_target_pairs={{0,2},{2,0},{4,6},{6,4},{8,10},{10,8},{12,14},{14,12},{16,18},{18,... | collective-permute-start | bytes 196616 | tf_op jit(solution)/shard_map/ppermute | solution.py:18
  12.2 8.8 %collective-permute-start.2 = (bf16[64,4,128]{0,2,1:T(8,128)(2,1)S(1)}, bf16[64,4,128]{0,2,1:T(8,128)(2,1)}, u32[]{:S(2)}, u32[]{:S(2)}) collective-permute-start(bf16[64,4,128]{0,2,1:T(8,128)(2,1)S(1)} %bitcast.93), channel_id=1, source_target_pairs={{0,2},{2,0},{4,6},{6,4},{8,10},{10,8},{12,14},{14,12},{16,18},{18,... | collective-permute-start | bytes 196616 | tf_op jit(solution)/shard_map/ppermute | solution.py:18
  14.9 1.1 copy-start.1
  32.3 6.0 %slice-start = ((s8[5242880]{0:T(1024)(128)(4,1)}), s8[1048576]{0:T(1024)(128)(4,1)S(1)}, s32[]{:S(2)}) async-start(s8[5242880]{0:T(1024)(128)(4,1)} %bitcast.84), calls=%async_computation.2 | async-start | bytes 2097152 | tf_op jit(solution)/shard_map/while
  32.4 5.9 %slice-start.1 = ((s8[5242880]{0:T(1024)(128)(4,1)}), s8[4194304]{0:T(1024)(128)(4,1)S(1)}, s32[]{:S(2)}) async-start(s8[5242880]{0:T(1024)(128)(4,1)} %bitcast.84), calls=%async_computation.3 | async-start | bytes 8388608 | tf_op jit(solution)/shard_map/while
  48.7 5.9 %slice-start = ((s8[5242880]{0:T(1024)(128)(4,1)}), s8[1048576]{0:T(1024)(128)(4,1)S(1)}, s32[]{:S(2)}) async-start(s8[5242880]{0:T(1024)(128)(4,1)} %bitcast.84), calls=%async_computation.2 | async-start | bytes 2097152 | tf_op jit(solution)/shard_map/while
  48.8 5.7 %slice-start.1 = ((s8[5242880]{0:T(1024)(128)(4,1)}), s8[4194304]{0:T(1024)(128)(4,1)S(1)}, s32[]{:S(2)}) async-start(s8[5242880]{0:T(1024)(128)(4,1)} %bitcast.84), calls=%async_computation.3 | async-start | bytes 8388608 | tf_op jit(solution)/shard_map/while
  64.9 6.0 %slice-start = ((s8[5242880]{0:T(1024)(128)(4,1)}), s8[1048576]{0:T(1024)(128)(4,1)S(1)}, s32[]{:S(2)}) async-start(s8[5242880]{0:T(1024)(128)(4,1)} %bitcast.84), calls=%async_computation.2 | async-start | bytes 2097152 | tf_op jit(solution)/shard_map/while
  65.0 5.8 %slice-start.1 = ((s8[5242880]{0:T(1024)(128)(4,1)}), s8[4194304]{0:T(1024)(128)(4,1)S(1)}, s32[]{:S(2)}) async-start(s8[5242880]{0:T(1024)(128)(4,1)} %bitcast.84), calls=%async_computation.3 | async-start | bytes 8388608 | tf_op jit(solution)/shard_map/while
  81.3 6.1 %slice-start = ((s8[5242880]{0:T(1024)(128)(4,1)}), s8[1048576]{0:T(1024)(128)(4,1)S(1)}, s32[]{:S(2)}) async-start(s8[5242880]{0:T(1024)(128)(4,1)} %bitcast.84), calls=%async_computation.2 | async-start | bytes 2097152 | tf_op jit(solution)/shard_map/while
  81.4 5.9 %slice-start.1 = ((s8[5242880]{0:T(1024)(128)(4,1)}), s8[4194304]{0:T(1024)(128)(4,1)S(1)}, s32[]{:S(2)}) async-start(s8[5242880]{0:T(1024)(128)(4,1)} %bitcast.84), calls=%async_computation.3 | async-start | bytes 8388608 | tf_op jit(solution)/shard_map/while
  89.3 2.8 %collective-permute-start.3 = (bf16[4,5,64]{2,1,0:T(8,128)(2,1)S(1)}, bf16[4,5,64]{2,1,0:T(8,128)(2,1)S(1)}, u32[]{:S(2)}, u32[]{:S(2)}) collective-permute-start(bf16[4,5,64]{2,1,0:T(8,128)(2,1)S(1)} %dynamic-slice_convert_fusion.2), channel_id=1, source_target_pairs={{0,2},{2,0},{4,6},{6,4},{8,10},{10,8},{12,14},{14,12},{16,18},{18,... | collective-permute-start | bytes 7688 | tf_op jit(solution)/shard_map/ppermute | solution.py:18
  91.4 1.8 collective-permute-start.4
  91.8 1.4 collective-permute-start.5
Sparse Core Ops, SparseCore 0:
  9.0 136.2 all-gather.1
  159.1 31.4 all-reduce.2
where the time goes:
time: 200 us; the launch traced here: 199 us
  waiting for transfers between devices  84.2 us (42%)
  matrix products  54.7 us (27%)
  local copies, waits for them, and re-layouts  29 us (14%)
  between operations  15 us (8%)
  other arithmetic  13.9 us (7%)
    all_gather x1, waiting for transfers between devices, shards(): lax.all_gather(w_out, 'req', axis=0, tiled=True)  50.8 us
    psum x1, waiting for transfers between devices, tensor_total(): return lax.psum(partial_value.astype(jnp.bfloat16), 'tp')  31.6 us
    dot_general x5, matrix products, absorb(): jnp.einsum('cgqk,kcd->qcgd', weights.astype(jnp.bfloat16), block_values,...  25.9 us
    dot_general x5, matrix products, absorb(): jnp.einsum('qcgd,kcd->cgqk', queries, block_keys, preferred_element_type=...  15.1 us
    dot_general x1, matrix products, shards(): lax.dot_general(attention, lax.all_gather(w_out, 'req', axis=0, tiled=Tru...  13.7 us
    gather x4, local copies, waits for them, and re-layouts, visit(): block_values = v_cache[slots].reshape(block_rows, local_heads, HD)  8.77 us
    gather x4, local copies, waits for them, and re-layouts, visit(): block_keys = k_cache[slots].reshape(block_rows, local_heads, HD)  8.76 us
    reduce_sum x5, other arithmetic, absorb(): running_sum = running_sum * factor + jnp.sum(weights, axis=-1)  6.95 us
  transfers between devices with their start and end apart: 8, of which 3 were waited for; matrix products, arithmetic and copies ran while one was open for 41% of the time, Pallas kernels for 0%

commit v1 on v0

v1 whole, which is shorter than its diff:
```python
import math

import jax
import jax.numpy as jnp
from jax import lax
from jax.experimental import pallas as pl
from jax.experimental.pallas import tpu as pltpu
from jax.sharding import PartitionSpec as P

HD = 128
GROUP = 5
CHUNK = 512
ROPE_BASE = 1000000.0
FLOOR_SCORE = -1e30
LOG2E = 1.4426950408889634


def from_partner(value, axis):
    return lax.ppermute(value, axis, [(i, i ^ 1) for i in range(lax.axis_size(axis))])


def turn(x, cosine, sine):
    x = x.astype(jnp.float32)
    return (x * cosine + pltpu.roll(x, HD // 2, 1) * sine).astype(jnp.bfloat16)


def attend(rows, q_own, q_peer, k_own, v_own, kc, vc, cos_ref, sin_ref, bias, fresh_bias, o_ref, lse_ref):
    c = LOG2E / math.sqrt(HD)
    parts = []
    for g in range(GROUP):
        cut = slice(g * HD, (g + 1) * HD)
        parts.append(turn(q_own[:, cut], cos_ref[:rows], sin_ref[:rows]))
        parts.append(turn(q_peer[:, cut], cos_ref[rows:], sin_ref[rows:]))
    q = jnp.concatenate(parts, axis=0)
    keys = turn(k_own[...], cos_ref[:rows], sin_ref[:rows])
    dims = (((1,), (1,)), ((), ()))
    s = lax.dot_general(q, keys, dims, preferred_element_type=jnp.float32) * c
    s = s + jnp.concatenate([fresh_bias[...]] * GROUP, axis=0)
    m = jnp.max(s, axis=1, keepdims=True)
    p = jnp.exp2(s - m)
    l = jnp.sum(p, axis=1, keepdims=True)
    o = jnp.dot(p.astype(jnp.bfloat16), v_own[...], preferred_element_type=jnp.float32)
    for first in range(0, kc.shape[0], CHUNK):
        cut = slice(first, first + CHUNK)
        s = lax.dot_general(q, kc[cut], dims, preferred_element_type=jnp.float32) * c + bias[:, cut]
        top = jnp.maximum(m, jnp.max(s, axis=1, keepdims=True))
        factor = jnp.exp2(m - top)
        m = top
        p = jnp.exp2(s - m)
        l = l * factor + jnp.sum(p, axis=1, keepdims=True)
        o = o * factor + jnp.dot(p.astype(jnp.bfloat16), vc[cut], preferred_element_type=jnp.float32)
    o = (o / l).astype(jnp.bfloat16)
    lse = m + jnp.log2(l)
    for g in range(GROUP):
        o_ref[:, g * HD : (g + 1) * HD] = o[g * 2 * rows : (g + 1) * 2 * rows]
        lse_ref[:, g : g + 1] = lse[g * 2 * rows : (g + 1) * 2 * rows]


def tables(q_new, k_cache, lengths, page_table):
    rows = q_new.shape[0]
    pages, page_rows = k_cache.shape[0], k_cache.shape[1]
    device_row = lax.axis_index("req")
    parity = device_row % 2
    request = device_row // 2
    length = lengths[request]
    token = (jnp.arange(2 * rows) + parity * rows) % (2 * rows)
    inverse = 1.0 / ROPE_BASE ** (jnp.arange(0, HD, 2).astype(jnp.float32) / HD)
    angles = (length + token).astype(jnp.float32)[:, None] * inverse[None, :]
    cosine = jnp.concatenate([jnp.cos(angles)] * 2, axis=-1)
    sine = jnp.sin(angles)
    sine = jnp.concatenate([-sine, sine], axis=-1)
    slot = device_row * pages + jnp.arange(pages)
    same = page_table[request][None, :] == slot[:, None]
    logical = jnp.max(jnp.where(same, jnp.arange(page_table.shape[1])[None, :], -1), axis=1)
    place = logical[:, None] * page_rows + jnp.arange(page_rows)[None, :]
    usable = (logical >= 0)[:, None] & (place < length)
    bias = jnp.where(usable, 0.0, FLOOR_SCORE).astype(jnp.float32).reshape(1, pages * page_rows)
    fresh = token[None, :rows] <= token[:, None]
    fresh_bias = jnp.where(fresh, 0.0, FLOOR_SCORE).astype(jnp.float32)
    return cosine, sine, bias, fresh_bias


def shards(q_new, k_new, v_new, k_cache, v_cache, lengths, page_table, w_out):
    rows = q_new.shape[0]
    heads = k_new.shape[1] // HD
    keys = k_cache.shape[0] * k_cache.shape[1]
    peer_q = from_partner(q_new, "req")
    cosine, sine, bias, fresh_bias = tables(q_new, k_cache, lengths, page_table)
    wide = GROUP * HD
    whole = lambda shape: pl.BlockSpec(shape, lambda h: (0, 0))
    by_head = lambda n, w: pl.BlockSpec((n, w), lambda h: (0, h))
    o, lse = pl.pallas_call(
        lambda *refs: attend(rows, *refs),
        grid=(heads,),
        in_specs=[
            by_head(rows, wide),
            by_head(rows, wide),
            by_head(rows, HD),
            by_head(rows, HD),
            by_head(keys, HD),
            by_head(keys, HD),
            whole((2 * rows, HD)),
            whole((2 * rows, HD)),
            whole((1, keys)),
            whole((2 * rows, rows)),
        ],
        out_specs=[by_head(2 * rows, wide), by_head(2 * rows, HD)],
        out_shape=[
            jax.ShapeDtypeStruct((2 * rows, heads * wide), jnp.bfloat16),
            jax.ShapeDtypeStruct((2 * rows, heads * HD), jnp.float32),
        ],
        compiler_params=pltpu.CompilerParams(vmem_limit_bytes=48 * 2**20),
    )(
        q_new,
        peer_q,
        k_new,
        v_new,
        k_cache.reshape(keys, heads * HD),
        v_cache.reshape(keys, heads * HD),
        cosine,
        sine,
        bias,
        fresh_bias,
    )
    lse = lse.reshape(2 * rows, heads, HD)[:, :, :GROUP].reshape(2 * rows, heads * GROUP)
    other_o = from_partner(o[rows:], "req")
    other_lse = from_partner(lse[rows:], "req")
    share = 1.0 / (1.0 + jnp.exp2(other_lse - lse[:rows]))
    share = share[:, :, None]
    mine = o[:rows].reshape(rows, heads * GROUP, HD).astype(jnp.float32)
    theirs = other_o.reshape(rows, heads * GROUP, HD).astype(jnp.float32)
    attention = (mine * share + theirs * (1.0 - share)).astype(jnp.bfloat16)
    gathered = lax.all_gather(attention.reshape(rows, heads * wide), "req", axis=0, tiled=True)
    part = lax.dot_general(
        gathered, w_out, (((1,), (1,)), ((), ())), preferred_element_type=jnp.float32
    ).astype(jnp.bfloat16)
    part = lax.all_to_all(part, "req", split_axis=0, concat_axis=1, tiled=True)
    return lax.psum(part, "tp")


def solution(mesh):
    in_specs = (
        P("req", "tp"),
        P("req", "tp"),
        P("req", "tp"),
        P("req", None, "tp"),
        P("req", None, "tp"),
        P(),
        P(),
        P("req", "tp"),
    )
    return jax.shard_map(
        shards, mesh=mesh, in_specs=in_specs, out_specs=P("req", None), check_vma=False
    )
```

time: 200 us -> 160 us (0.80)
  matrix products: 54.7 us -> 4.36 us
  blocking collectives: 0 us -> 23.4 us
  local copies, waits for them, and re-layouts: 29 us -> 13 us
  Pallas kernels: 0 us -> 11.1 us
  other arithmetic: 13.9 us -> 3.07 us
  waiting for transfers between devices: 84.2 us -> 90.4 us
    dot_general x11 -> x1, matrix products: 54.7 us -> 4.36 us  [shards(): lax.dot_general(gathered, w_out, (((1,), (1,)), ((), ())), preferred_elem...]
    all_to_all x0 -> x1, blocking collectives: none -> 23.4 us  [shards(): part = lax.all_to_all(part, 'req', split_axis=0, concat_axis=1, tiled=True)]
    gather x8 -> x0, local copies, waits for them, and re-layouts: 17.5 us -> none  [the longest x4 8.77 us: visit(): block_values = v_cache[slots].reshape(block_rows, local_heads, HD)]
    pallas_call x0 -> x1, Pallas kernels: none -> 11.1 us  [shards(): pl.pallas_call(lambda *refs: attend(rows, *refs), grid=(heads,), in_specs...]
    all_gather x1, waiting for transfers between devices: 50.8 us -> 58.5 us  [shards(): lax.all_gather(attention.reshape(rows, heads * wide), 'req', axis=0, tile...]
    reduce_sum x5 -> x0, other arithmetic: 6.95 us -> none  [absorb(): running_sum = running_sum * factor + jnp.sum(weights, axis=-1)]
    unnamed x13, local copies, waits for them, and re-layouts: 2.84 us -> 7.8 us
    and x5 -> x0, other arithmetic: 2.55 us -> none  [the longest x4 2.53 us: visit(): usable = jnp.repeat(logical < last_page, page_rows) & (key_places < length)]
  transfers between devices with their start and end apart: 8 -> 5, of which waited for: 3 -> 3; matrix products, arithmetic and copies ran while one was open for 41% -> 3% of each run, Pallas kernels for 0% -> 0%
where the time goes in v1:
time: 160 us
  waiting for transfers between devices  90.4 us (56%)
  blocking collectives  23.4 us (15%)
  between operations  13.5 us (8%)
  local copies, waits for them, and re-layouts  13 us (8%)
  Pallas kernels  11.1 us (7%)
  matrix products  4.36 us (3%)
  other arithmetic  3.07 us (2%)
    all_gather x1, waiting for transfers between devices, shards(): lax.all_gather(attention.reshape(rows, heads * wide), 'req', axis=0, tile...  58.5 us
    psum x1, waiting for transfers between devices, shards(): return lax.psum(part, 'tp')  30.8 us
    all_to_all x1, blocking collectives, shards(): part = lax.all_to_all(part, 'req', split_axis=0, concat_axis=1, tiled=True)  23.4 us
    pallas_call x1, Pallas kernels, shards(): pl.pallas_call(lambda *refs: attend(rows, *refs), grid=(heads,), in_specs...  11.1 us
    unnamed x13, local copies, waits for them, and re-layouts  7.8 us
    dot_general x1, matrix products, shards(): lax.dot_general(gathered, w_out, (((1,), (1,)), ((), ())), preferred_elem...  4.36 us
  transfers between devices with their start and end apart: 5, of which 3 were waited for; matrix products, arithmetic and copies ran while one was open for 3% of the time, Pallas kernels for 0%

profile of v1, /device:TPU:0, one launch (start us, length us, event | category | flops | bytes accessed | tf_op | source)
XLA Modules:
  0.0 159.9 jit_solution(13768529553862542925)
XLA Ops:
  6.5 0.0 copy-start
  6.5 0.0 all-gather.2.cloned.1.call-start
  6.5 0.5 collective-permute-start
  7.0 0.7 dynamic-slice_bitcast_fusion
  7.7 0.2 select_reduce_fusion
  7.9 1.2 dynamic_slice.6
  9.2 0.7 add_convert_fusion
  9.9 0.7 fusion.4
  10.6 0.3 fusion.2
  10.9 0.1 pad_maximum_fusion
  11.0 0.1 compare_select_fusion.refs_9_
  11.1 0.0 collective-permute-done.refs_1_
  11.1 0.0 copy-start.1
  11.1 1.6 copy-done.1
  12.7 0.0 copy-start.2
  12.7 1.6 copy-done.2
  14.3 0.0 copy-start.3
  14.3 1.0 copy-done.3
  15.3 0.0 copy-start.4
  15.3 0.8 copy-done.4
  16.1 0.0 copy-start.5
  16.1 0.8 copy-done.5
  17.0 11.1 %shard_map.82 = (bf16[128,2560]{1,0:T(8,128)(2,1)S(1)}, f32[128,512]{1,0:T(8,128)S(1)}) custom-call(bf16[64,2560]{1,0:T(8,128)(2,1)S(1)} %copy-done.3, bf16[64,2560]{1,0:T(8,128)(2,1)S(1)} %collective-permute-done.refs_1_, bf16[64,512]{1,0:T(8,128)(2,1)S(1)} %copy-done.4, bf16[64,512]{1,0:T(8,128)(2,1)S(1)} %copy-done.5, bf16[2048,512]{1,0:T(8,128)(2,1)S(1)} %bitcast.28, ...), custom_call_target="tpu_custom_call" | custom-call | tf_op jit(solution)/shard_map/pallas_call | solution.py:92
  28.1 0.1 copy.27
  28.2 0.2 collective-permute-start.2
  28.4 0.1 fusion.6
  28.5 0.4 collective-permute-start.1
  28.9 1.1 collective-permute-done.1
  30.0 0.1 copy.24
  30.0 0.1 copy.23
  30.1 0.0 collective-permute-done.2
  30.1 0.3 mul.67
  30.4 0.3 mul.70
  30.7 1.0 fusion.1
  31.7 0.0 all-gather.2.cloned.1.call-update
  31.7 0.0 all-reduce.2.cloned.1.call-start
  31.7 58.5 %all-gather.2.cloned.1.call-done = bf16[1024,2560]{1,0:T(8,128)(2,1)} async-done(((bf16[64,2560]{1,0:T(8,128)(2,1)}), bf16[1024,2560]{1,0:T(8,128)(2,1)}) %all-gather.2.cloned.1.call-update) | async-done | bytes 5242896 | tf_op jit(solution)/shard_map/all_gather | solution.py:133
  90.2 0.0 copy-done
  90.2 4.4 %convolution_convert_fusion = bf16[1024,320]{0,1:T(8,128)(2,1)S(1)} fusion(bf16[1024,2560]{1,0:T(8,128)(2,1)} %all-gather.2.cloned.1.call-done, bf16[320,2560]{1,0:T(8,128)(2,1)S(1)} %copy-done), kind=kOutput, calls=%fused_computation | convolution fusion | flops 1678049280 | bytes 7536640 | tf_op jit(solution)/shard_map/dot_general | solution.py:134
  94.6 0.4 copy.25
  94.9 23.4 %all_to_all.19 = bf16[16,64,320]{2,1,0:T(8,128)(2,1)S(1)} all-to-all(bf16[16,64,320]{2,1,0:T(8,128)(2,1)S(1)} %bitcast.34), channel_id=1, replica_groups=mesh['req'=16,'tp'=2] {'req'}, dimensions={0} | all-to-all | bytes 1310720 | tf_op jit(solution)/shard_map/all_to_all | solution.py:137
  118.3 0.5 copy.26
  118.8 1.5 all_to_all.17
  120.3 0.0 all-reduce.2.cloned.1.call-update
  120.3 30.8 %all-reduce.2.cloned.1.call-done = bf16[64,5120]{1,0:T(8,128)(2,1)} async-done(((bf16[64,5120]{1,0:T(8,128)(2,1)}), bf16[64,5120]{1,0:T(8,128)(2,1)}) %all-reduce.2.cloned.1.call-update) | async-done | bytes 655376 | tf_op jit(solution)/shard_map/psum | solution.py:138
  151.1 2.0 %copy.33 = bf16[64,5120]{1,0:T(8,128)(2,1)} copy(bf16[64,5120]{1,0:T(8,128)(2,1)} %all-reduce.2.cloned.1.call-done) | data formatting | bytes 1310720
  (9 shorter events, 0.1 us)
Async XLA Ops:
  6.5 83.7 %copy-start = (bf16[320,2560]{1,0:T(8,128)(2,1)S(1)}, bf16[320,2560]{1,0:T(8,128)(2,1)}, u32[]{:S(2)}) copy-start(bf16[320,2560]{1,0:T(8,128)(2,1)} %param.15) | copy-start | bytes 4915204
  6.5 83.7 %all-gather.2.cloned.1.call-start = ((), (), s32[]{:S(2)}) async-start(), calls=%async_computation.1 | async-start | bytes 5570560 | tf_op jit(solution)/shard_map/all_gather | solution.py:133
  6.5 4.6 %collective-permute-start = (bf16[64,2560]{1,0:T(8,128)(2,1)}, bf16[64,2560]{1,0:T(8,128)(2,1)S(1)}, u32[]{:S(2)}, u32[]{:S(2)}) collective-permute-start(bf16[64,2560]{1,0:T(8,128)(2,1)} %refs_0_.1), channel_id=1, source_target_pairs={{0,2},{2,0},{4,6},{6,4},{8,10},{10,8},{12,14},{14,12},{16,18},{18,... | collective-permute-start | bytes 983048 | tf_op jit(solution)/shard_map/ppermute | solution.py:19
  11.1 1.6 copy-start.1
  12.7 1.6 copy-start.2
  14.3 1.0 copy-start.3
  15.3 0.8 copy-start.4
  16.1 0.8 copy-start.5
  28.2 1.9 %collective-permute-start.2 = (bf16[64,2560]{1,0:T(8,128)(2,1)S(1)}, bf16[64,2560]{1,0:T(8,128)(2,1)S(1)}, u32[]{:S(2)}, u32[]{:S(2)}) collective-permute-start(bf16[64,2560]{1,0:T(8,128)(2,1)S(1)} %slice.30), channel_id=1, source_target_pairs={{0,2},{2,0},{4,6},{6,4},{8,10},{10,8},{12,14},{14,12},{16,18},{18,... | collective-permute-start | bytes 983048 | tf_op jit(solution)/shard_map/ppermute | solution.py:19
  28.5 1.4 collective-permute-start.1
  31.7 119.4 %all-reduce.2.cloned.1.call-start = ((), (), s32[]{:S(2)}) async-start(), calls=%async_computation.2 | async-start | bytes 1310720 | tf_op jit(solution)/shard_map/psum | solution.py:138
Sparse Core Ops, SparseCore 0:
  31.8 58.3 all-gather.1
  120.4 30.6 all-reduce.1

commit v2 on v1

--- a/solution.py
+++ b/solution.py
@@ -54,6 +54,188 @@
     for g in range(GROUP):
         o_ref[:, g * HD : (g + 1) * HD] = o[g * 2 * rows : (g + 1) * 2 * rows]
         lse_ref[:, g : g + 1] = lse[g * 2 * rows : (g + 1) * 2 * rows]
+
+
+def project_kernel(n, att, w, out, gat, part, ybuf, red, ring_s, ring_r, core_s, core_r, y_s, y_r, sc_s, sc_r, f_s, f_r):
+    chips = n // 2
+    side = chips // 2
+    me = lax.axis_index("req")
+    t = lax.axis_index("tp")
+    core = me % 2
+    chip = me // 2
+    column = chip % 2
+    place = (1 - column) * (chip // 2) + column * (chips - 1 - chip // 2)
+
+    def chip_at(offset):
+        pos = (place + offset + chips) % chips
+        far = pos // side
+        return (1 - far) * 2 * pos + far * (2 * (chips - 1 - pos) + 1)
+
+    peer = me + 1 - 2 * core
+    barrier = pltpu.get_barrier_semaphore()
+    for k in range(1, n):
+        pl.semaphore_signal(
+            barrier, inc=1, device_id=((me + k) % n, t), device_id_type=pl.DeviceIdType.MESH
+        )
+    pl.semaphore_signal(barrier, inc=1, device_id=(me, 1 - t), device_id_type=pl.DeviceIdType.MESH)
+    pl.semaphore_wait(barrier, n)
+
+    def remote(src, dst, s, r, row, col):
+        return pltpu.make_async_remote_copy(
+            src_ref=src, dst_ref=dst, send_sem=s, recv_sem=r,
+            device_id=(row, col), device_id_type=pl.DeviceIdType.MESH,
+        )
+
+    gat[me] = att[...]
+    left = chip_at(-1) * 2 + core
+    right = chip_at(1) * 2 + core
+    steps_up = chips // 2
+    steps_down = chips - 1 - steps_up
+
+    def ring(d, j, to):
+        block = chip_at(j if d == 0 else -j) * 2 + core
+        slot = d * chips + j
+        return remote(gat.at[block], gat.at[block], ring_s.at[slot], ring_r.at[slot], to, t)
+
+    def cross(offset):
+        block = chip_at(offset) * 2 + core
+        slot = offset % chips
+        return remote(gat.at[block], gat.at[block], core_s.at[slot], core_r.at[slot], peer, t)
+
+    sent = []
+
+    def start(copy):
+        copy.start()
+        sent.append(copy)
+
+    start(ring(0, 0, left))
+    start(ring(1, 0, right))
+    start(cross(0))
+
+    def trade(offset):
+        c = chip_at(offset)
+        slot = offset % chips
+        return remote(part.at[c, 1 - t], ybuf.at[c], y_s.at[slot], y_r.at[slot], me, 1 - t)
+
+    def multiply(offset):
+        c = chip_at(offset)
+        cross(offset).wait_recv()
+        rows = gat.shape[1]
+        half = rows // 2
+        for k in range(2):
+            got = lax.dot_general(
+                gat[2 * c + k], w[...], (((1,), (1,)), ((), ())), preferred_element_type=jnp.float32
+            ).astype(jnp.bfloat16)
+            part[c, 0, k] = got[:half]
+            part[c, 1, k] = got[half:]
+        start(trade(offset))
+
+    def scatter(offset, k):
+        slot = (offset % chips) * 2 + k
+        c = chip_at(offset)
+        dev = 2 * c + (core + k) % 2
+        return remote(red.at[c, (core + k) % 2], out.at[me, t], sc_s.at[slot], sc_r.at[slot], dev, t)
+
+    def reduce(offset):
+        c = chip_at(offset)
+        trade(offset).wait_recv()
+        total = part[c, t].astype(jnp.float32) + ybuf[c].astype(jnp.float32)
+        red[c] = total.astype(jnp.bfloat16)
+        if offset == 0:
+            out[me, t] = red[c, core]
+        else:
+            start(scatter(offset, 0))
+        start(scatter(offset, 1))
+
+    def forward(offset, k):
+        slot = (offset % chips) * 2 + k
+        dev = chip_at(offset) * 2 + (core + k) % 2
+        return remote(out.at[dev, t], out.at[dev, t], f_s.at[slot], f_r.at[slot], me, 1 - t)
+
+    def landed(offset, k):
+        slot = ((-offset) % chips) * 2 + k
+        dev = chip_at(offset) * 2 + (core + k) % 2
+        return remote(red.at[0, 0], out.at[dev, t], sc_s.at[slot], sc_r.at[slot], dev, t)
+
+    def collect(offset):
+        for k in range(2):
+            if offset != 0 or k == 1:
+                landed(offset, k).wait_recv()
+            start(forward(offset, k))
+
+    order = [0]
+    for j in range(1, steps_up + 1):
+        order.append(j)
+        if j <= steps_down:
+            order.append(-j)
+    done = 0
+    for j in range(1, steps_up + 1):
+        remote(gat.at[0], gat.at[chip_at(j) * 2 + core], ring_s.at[j - 1], ring_r.at[j - 1], left, t).wait_recv()
+        if j < steps_up:
+            start(ring(0, j, left))
+        start(cross(j))
+        if j <= steps_down:
+            slot = chips + j - 1
+            remote(gat.at[0], gat.at[chip_at(-j) * 2 + core], ring_s.at[slot], ring_r.at[slot], right, t).wait_recv()
+            if j < steps_down:
+                start(ring(1, j, right))
+            start(cross(-j))
+        ready = 1 if j == 1 else 2 * j - 1
+        while done < min(ready, len(order)):
+            multiply(order[done])
+            if done >= 1:
+                reduce(order[done - 1])
+            done += 1
+    while done < len(order):
+        multiply(order[done])
+        reduce(order[done - 1])
+        done += 1
+    reduce(order[-1])
+    for offset in order:
+        collect(offset)
+    for offset in order:
+        for k in range(2):
+            dev = chip_at(offset) * 2 + (core + k) % 2
+            slot = (offset % chips) * 2 + k
+            remote(red.at[0, 0], out.at[dev, 1 - t], f_s.at[slot], f_r.at[slot], me, 1 - t).wait_recv()
+    for copy in sent:
+        copy.wait_send()
+
+
+def project(attention, w_out):
+    n = lax.axis_size("req")
+    rows, deep = attention.shape
+    cols = w_out.shape[0]
+    chips = n // 2
+    half = rows // 2
+    dma = pltpu.SemaphoreType.DMA
+    vmem = pl.BlockSpec(memory_space=pltpu.VMEM)
+    out = pl.pallas_call(
+        lambda *refs: project_kernel(n, *refs),
+        in_specs=[vmem, vmem],
+        out_specs=vmem,
+        out_shape=jax.ShapeDtypeStruct((n, 2, half, cols), jnp.bfloat16),
+        scratch_shapes=[
+            pltpu.VMEM((n, rows, deep), jnp.bfloat16),
+            pltpu.VMEM((chips, 2, 2, half, cols), jnp.bfloat16),
+            pltpu.VMEM((chips, 2, half, cols), jnp.bfloat16),
+            pltpu.VMEM((chips, 2, half, cols), jnp.bfloat16),
+            dma((2 * chips,)),
+            dma((2 * chips,)),
+            dma((chips,)),
+            dma((chips,)),
+            dma((chips,)),
+            dma((chips,)),
+            dma((n,)),
+            dma((n,)),
+            dma((n,)),
+            dma((n,)),
+        ],
+        compiler_params=pltpu.CompilerParams(
+            collective_id=0, has_side_effects=True, vmem_limit_bytes=40 * 2**20
+        ),
+    )(attention, w_out)
+    return jnp.transpose(out.reshape(n, rows, cols), (1, 0, 2)).reshape(rows, n * cols)
 
 
 def tables(q_new, k_cache, lengths, page_table):
@@ -130,7 +312,10 @@
     mine = o[:rows].reshape(rows, heads * GROUP, HD).astype(jnp.float32)
     theirs = other_o.reshape(rows, heads * GROUP, HD).astype(jnp.float32)
     attention = (mine * share + theirs * (1.0 - share)).astype(jnp.bfloat16)
-    gathered = lax.all_gather(attention.reshape(rows, heads * wide), "req", axis=0, tiled=True)
+    attention = attention.reshape(rows, heads * wide)
+    if lax.axis_size("tp") == 2 and rows % 32 == 0 and lax.axis_size("req") % 4 == 0:
+        return project(attention, w_out)
+    gathered = lax.all_gather(attention, "req", axis=0, tiled=True)
     part = lax.dot_general(
         gathered, w_out, (((1,), (1,)), ((), ())), preferred_element_type=jnp.float32
     ).astype(jnp.bfloat16)

time: 160 us -> 84.1 us (0.53)
  waiting for transfers between devices: 90.4 us -> 1.14 us
  Pallas kernels: 11.1 us -> 68.2 us
  blocking collectives: 23.4 us -> 0 us
  between operations: 13.5 us -> 0.14 us
  matrix products: 4.36 us -> 0 us
  local copies, waits for them, and re-layouts: 13 us -> 10.8 us
    all_gather x1 -> x0, waiting for transfers between devices: 58.5 us -> none  [shards(): lax.all_gather(attention.reshape(rows, heads * wide), 'req', axis=0, tile...]
    pallas_call x0 -> x1, Pallas kernels: none -> 57.1 us  [project(): pl.pallas_call(lambda *refs: project_kernel(n, *refs), in_specs=[vmem, vm...]
    psum x1 -> x0, waiting for transfers between devices: 30.8 us -> none  [shards(): return lax.psum(part, 'tp')]
    all_to_all x1 -> x0, blocking collectives: 23.4 us -> none  [shards(): part = lax.all_to_all(part, 'req', split_axis=0, concat_axis=1, tiled=True)]
    dot_general x1 -> x0, matrix products: 4.36 us -> none  [shards(): lax.dot_general(gathered, w_out, (((1,), (1,)), ((), ())), preferred_elem...]
    all_to_all x2 -> x0, local copies, waits for them, and re-layouts: 1.93 us -> none  [shards(): part = lax.all_to_all(part, 'req', split_axis=0, concat_axis=1, tiled=True)]
    unnamed x13 -> x14, local copies, waits for them, and re-layouts: 7.8 us -> 6.69 us
  transfers between devices with their start and end apart: 5 -> 3, of which waited for: 3 -> 1; matrix products, arithmetic and copies ran while one was open for 3% -> 4% of each run, Pallas kernels for 0% -> 0%
where the time goes in v2:
time: 84.1 us; the launch traced here: 83.7 us
  Pallas kernels  68.2 us (81%)
  local copies, waits for them, and re-layouts  10.8 us (13%)
  other arithmetic  2.35 us (3%)
  waiting for transfers between devices  1.14 us (1%)
  starting transfers between devices  1.03 us (1%)
    pallas_call x1, Pallas kernels, project(): pl.pallas_call(lambda *refs: project_kernel(n, *refs), in_specs=[vmem, vm...  57.1 us
    pallas_call x1, Pallas kernels, shards(): pl.pallas_call(lambda *refs: attend(rows, *refs), grid=(heads,), in_specs...  11.1 us
    unnamed x14, local copies, waits for them, and re-layouts  6.69 us
  transfers between devices with their start and end apart: 3, of which 1 were waited for; matrix products, arithmetic and copies ran while one was open for 4% of the time, Pallas kernels for 0%

profile of v2, /device:TPU:0, one launch (start us, length us, event | category | flops | bytes accessed | tf_op | source)
XLA Modules:
  0.0 83.7 jit_solution(17635080860889726716)
XLA Ops:
  0.0 0.0 copy-start
  0.0 0.5 collective-permute-start
  0.5 0.2 copy-done
  0.7 0.2 select_reduce_fusion
  0.9 1.2 %dynamic_slice.6 = s32[1]{0:T(128)} dynamic-slice(s32[8]{0:T(128)} %param.13, s32[]{:T(128)S(6)} %select_n.51), dynamic_slice_sizes={1} | dynamic-slice | bytes 12 | tf_op jit(solution)/shard_map/dynamic_slice | solution.py:247
  2.2 0.7 add_convert_fusion
  2.8 0.7 fusion.4
  3.5 0.3 fusion.2
  3.9 0.1 pad_maximum_fusion
  4.0 0.1 compare_select_fusion.refs_9_
  4.1 0.0 collective-permute-done.refs_1_
  4.1 0.0 copy-start.1
  4.1 1.6 %copy-done.1 = bf16[16,128,512]{2,1,0:T(8,128)(2,1)S(1)} copy-done((bf16[16,128,512]{2,1,0:T(8,128)(2,1)S(1)}, bf16[16,128,512]{2,1,0:T(8,128)(2,1)}, u32[]{:S(2)}) %copy-start.1) | copy-done | bytes 2097176
  5.7 0.0 copy-start.2
  5.7 1.6 %copy-done.2 = bf16[16,128,512]{2,1,0:T(8,128)(2,1)S(1)} copy-done((bf16[16,128,512]{2,1,0:T(8,128)(2,1)S(1)}, bf16[16,128,512]{2,1,0:T(8,128)(2,1)}, u32[]{:S(2)}) %copy-start.2) | copy-done | bytes 2097176
  7.3 0.0 copy-start.4
  7.3 1.0 %copy-done.4 = bf16[64,2560]{1,0:T(8,128)(2,1)S(1)} copy-done((bf16[64,2560]{1,0:T(8,128)(2,1)S(1)}, bf16[64,2560]{1,0:T(8,128)(2,1)}, u32[]{:S(2)}) %copy-start.4) | copy-done | bytes 327704
  8.2 0.0 copy-start.5
  8.2 0.8 %copy-done.5 = bf16[64,512]{1,0:T(8,128)(2,1)S(1)} copy-done((bf16[64,512]{1,0:T(8,128)(2,1)S(1)}, bf16[64,512]{1,0:T(8,128)(2,1)}, u32[]{:S(2)}) %copy-start.5) | copy-done | bytes 65560
  9.1 0.0 copy-start.6
  9.1 0.8 %copy-done.6 = bf16[64,512]{1,0:T(8,128)(2,1)S(1)} copy-done((bf16[64,512]{1,0:T(8,128)(2,1)S(1)}, bf16[64,512]{1,0:T(8,128)(2,1)}, u32[]{:S(2)}) %copy-start.6) | copy-done | bytes 65560
  9.9 11.1 %shard_map.82 = (bf16[128,2560]{1,0:T(8,128)(2,1)S(1)}, f32[128,512]{1,0:T(8,128)S(1)}) custom-call(bf16[64,2560]{1,0:T(8,128)(2,1)S(1)} %copy-done.4, bf16[64,2560]{1,0:T(8,128)(2,1)S(1)} %collective-permute-done.refs_1_, bf16[64,512]{1,0:T(8,128)(2,1)S(1)} %copy-done.5, bf16[64,512]{1,0:T(8,128)(2,1)S(1)} %copy-done.6, bf16[2048,512]{1,0:T(8,128)(2,1)S(1)} %bitcast.28, ...), custom_call_target="tpu_custom_call" | custom-call | tf_op jit(solution)/shard_map/pallas_call | solution.py:274
  21.1 0.1 copy.20
  21.2 0.5 collective-permute-start.2
  21.7 0.1 fusion.6
  21.8 0.1 collective-permute-start.1
  21.9 1.1 %collective-permute-done.1 = f32[64,20]{0,1:T(8,128)S(1)} collective-permute-done((f32[64,20]{0,1:T(8,128)S(1)}, f32[64,20]{0,1:T(8,128)S(1)}, u32[]{:S(2)}, u32[]{:S(2)}) %collective-permute-start.1) | collective-permute-done | bytes 5152 | tf_op jit(solution)/shard_map/ppermute | solution.py:19
  23.0 0.1 copy.18
  23.1 0.1 copy.17
  23.2 0.0 copy-start.3
  23.2 0.0 collective-permute-done.2
  23.2 0.3 mul.67
  23.5 0.3 mul.70
  23.8 0.2 fusion.1.refs_0_
  24.0 0.6 copy-done.3
  24.6 57.1 %shard_map.83 = bf16[16,2,32,320]{3,2,1,0:T(8,128)(2,1)S(1)} custom-call(bf16[64,2560]{1,0:T(8,128)(2,1)S(1)} %fusion.1.refs_0_, bf16[320,2560]{1,0:T(8,128)(2,1)S(1)} %copy-done.3), custom_call_target="tpu_custom_call" | custom-call | tf_op jit(solution)/shard_map/pallas_call | solution.py:213
  81.7 0.5 copy.19
  82.2 1.5 %reshape.116 = bf16[64,5120]{1,0:T(8,128)(2,1)} reshape(bf16[64,16,320]{2,1,0:T(8,128)(2,1)S(1)} %copy.19) | data formatting | bytes 1310720 | tf_op jit(solution)/shard_map/reshape | solution.py:238
  (10 shorter events, 0.1 us)
Async XLA Ops:
  0.0 0.7 copy-start
  0.0 4.1 %collective-permute-start = (bf16[64,2560]{1,0:T(8,128)(2,1)}, bf16[64,2560]{1,0:T(8,128)(2,1)S(1)}, u32[]{:S(2)}, u32[]{:S(2)}) collective-permute-start(bf16[64,2560]{1,0:T(8,128)(2,1)} %refs_0_.1), channel_id=1, source_target_pairs={{0,2},{2,0},{4,6},{6,4},{8,10},{10,8},{12,14},{14,12},{16,18},{18,... | collective-permute-start | bytes 983048 | tf_op jit(solution)/shard_map/ppermute | solution.py:19
  4.1 1.6 %copy-start.1 = (bf16[16,128,512]{2,1,0:T(8,128)(2,1)S(1)}, bf16[16,128,512]{2,1,0:T(8,128)(2,1)}, u32[]{:S(2)}) copy-start(bf16[16,128,512]{2,1,0:T(8,128)(2,1)} %param.11) | copy-start | bytes 6291460
  5.7 1.6 %copy-start.2 = (bf16[16,128,512]{2,1,0:T(8,128)(2,1)S(1)}, bf16[16,128,512]{2,1,0:T(8,128)(2,1)}, u32[]{:S(2)}) copy-start(bf16[16,128,512]{2,1,0:T(8,128)(2,1)} %param.12) | copy-start | bytes 6291460
  7.3 1.0 %copy-start.4 = (bf16[64,2560]{1,0:T(8,128)(2,1)S(1)}, bf16[64,2560]{1,0:T(8,128)(2,1)}, u32[]{:S(2)}) copy-start(bf16[64,2560]{1,0:T(8,128)(2,1)} %refs_0_.1) | copy-start | bytes 983044
  8.2 0.8 %copy-start.5 = (bf16[64,512]{1,0:T(8,128)(2,1)S(1)}, bf16[64,512]{1,0:T(8,128)(2,1)}, u32[]{:S(2)}) copy-start(bf16[64,512]{1,0:T(8,128)(2,1)} %refs_2_.1) | copy-start | bytes 196612
  9.1 0.8 %copy-start.6 = (bf16[64,512]{1,0:T(8,128)(2,1)S(1)}, bf16[64,512]{1,0:T(8,128)(2,1)}, u32[]{:S(2)}) copy-start(bf16[64,512]{1,0:T(8,128)(2,1)} %refs_3_.1) | copy-start | bytes 196612
  21.2 2.0 %collective-permute-start.2 = (bf16[64,2560]{1,0:T(8,128)(2,1)S(1)}, bf16[64,2560]{1,0:T(8,128)(2,1)S(1)}, u32[]{:S(2)}, u32[]{:S(2)}) collective-permute-start(bf16[64,2560]{1,0:T(8,128)(2,1)S(1)} %slice.30), channel_id=1, source_target_pairs={{0,2},{2,0},{4,6},{6,4},{8,10},{10,8},{12,14},{14,12},{16,18},{18,... | collective-permute-start | bytes 983048 | tf_op jit(solution)/shard_map/ppermute | solution.py:19
  21.8 1.2 %collective-permute-start.1 = (f32[64,20]{0,1:T(8,128)S(1)}, f32[64,20]{0,1:T(8,128)S(1)}, u32[]{:S(2)}, u32[]{:S(2)}) collective-permute-start(f32[64,20]{0,1:T(8,128)S(1)} %slice.27), channel_id=1, source_target_pairs={{0,2},{2,0},{4,6},{6,4},{8,10},{10,8},{12,14},{14,12},{16,18},{18,... | collective-permute-start | bytes 15368 | tf_op jit(solution)/shard_map/ppermute | solution.py:19
  23.2 1.4 %copy-start.3 = (bf16[320,2560]{1,0:T(8,128)(2,1)S(1)}, bf16[320,2560]{1,0:T(8,128)(2,1)}, u32[]{:S(2)}) copy-start(bf16[320,2560]{1,0:T(8,128)(2,1)} %refs_1_.1) | copy-start | bytes 4915204

commit v3 on v2

--- a/solution.py
+++ b/solution.py
@@ -122,12 +122,13 @@
         cross(offset).wait_recv()
         rows = gat.shape[1]
         half = rows // 2
+        both = gat[pl.ds(2 * c, 2)].reshape(2 * rows, gat.shape[2])
+        got = lax.dot_general(
+            both, w[...], (((1,), (1,)), ((), ())), preferred_element_type=jnp.float32
+        ).astype(jnp.bfloat16)
         for k in range(2):
-            got = lax.dot_general(
-                gat[2 * c + k], w[...], (((1,), (1,)), ((), ())), preferred_element_type=jnp.float32
-            ).astype(jnp.bfloat16)
-            part[c, 0, k] = got[:half]
-            part[c, 1, k] = got[half:]
+            part[c, 0, k] = got[k * rows : k * rows + half]
+            part[c, 1, k] = got[k * rows + half : (k + 1) * rows]
         start(trade(offset))
 
     def scatter(offset, k):
@@ -185,13 +186,17 @@
             multiply(order[done])
             if done >= 1:
                 reduce(order[done - 1])
+            if done >= 4:
+                collect(order[done - 4])
             done += 1
     while done < len(order):
         multiply(order[done])
         reduce(order[done - 1])
+        if done >= 4:
+            collect(order[done - 4])
         done += 1
     reduce(order[-1])
-    for offset in order:
+    for offset in order[max(0, len(order) - 4) :]:
         collect(offset)
     for offset in order:
         for k in range(2):
@@ -291,7 +296,7 @@
             jax.ShapeDtypeStruct((2 * rows, heads * wide), jnp.bfloat16),
             jax.ShapeDtypeStruct((2 * rows, heads * HD), jnp.float32),
         ],
-        compiler_params=pltpu.CompilerParams(vmem_limit_bytes=48 * 2**20),
+        compiler_params=pltpu.CompilerParams(vmem_limit_bytes=60 * 2**20),
     )(
         q_new,
         peer_q,

time: 84.1 us -> 83.5 us (level)
  local copies, waits for them, and re-layouts: 10.8 us -> 7.71 us
  other arithmetic: 2.35 us -> 4.22 us
    unnamed x14 -> x8, local copies, waits for them, and re-layouts: 6.69 us -> 1.58 us
    pallas_call x1, Pallas kernels: 11.1 us -> 12.4 us  [shards(): pl.pallas_call(lambda *refs: attend(rows, *refs), grid=(heads,), in_specs...]
    reshape x1, local copies, waits for them, and re-layouts: 0.12 us -> 1.14 us  [shards(): lse.reshape(2 * rows, heads, HD)[:, :, :GROUP]]
    slice x1, local copies, waits for them, and re-layouts: 0.02 us -> 1 us  [shards(): other_o = from_partner(o[rows:], 'req')]
  transfers between devices with their start and end apart: 3 -> 3, of which waited for: 1 -> 1; matrix products, arithmetic and copies ran while one was open for 4% -> 7% of each run, Pallas kernels for 0% -> 0%
where the time goes in v3:
time: 83.5 us; the launch traced here: 83.2 us
  Pallas kernels  69 us (83%)
  local copies, waits for them, and re-layouts  7.71 us (9%)
  other arithmetic  4.22 us (5%)
  waiting for transfers between devices  1.14 us (1%)
  starting transfers between devices  1.03 us (1%)
    pallas_call x1, Pallas kernels, project(): pl.pallas_call(lambda *refs: project_kernel(n, *refs), in_specs=[vmem, vm...  56.6 us
    pallas_call x1, Pallas kernels, shards(): pl.pallas_call(lambda *refs: attend(rows, *refs), grid=(heads,), in_specs...  12.4 us
  transfers between devices with their start and end apart: 3, of which 1 were waited for; matrix products, arithmetic and copies ran while one was open for 7% of the time, Pallas kernels for 0%

profile of v3, /device:TPU:0, one launch (start us, length us, event | category | flops | bytes accessed | tf_op | source)
XLA Modules:
  0.0 83.2 jit_solution(15981682077433118453)
XLA Ops:
  0.0 0.0 copy-start
  0.0 0.5 collective-permute-start
  0.5 0.2 copy-done
  0.7 0.2 select_reduce_fusion
  0.9 1.2 %dynamic_slice.6 = s32[1]{0:T(128)} dynamic-slice(s32[8]{0:T(128)} %param.13, s32[]{:T(128)S(6)} %select_n.51), dynamic_slice_sizes={1} | dynamic-slice | bytes 12 | tf_op jit(solution)/shard_map/dynamic_slice | solution.py:252
  2.2 0.7 add_convert_fusion
  2.8 1.3 %fusion.4 = f32[16,128]{1,0:T(8,128)} fusion(s32[]{:T(128)} %bitcast.2, s32[16]{0:T(128)S(1)} %broadcast_multiply_fusion, pred[16]{0:T(512)(128)(4,1)S(1)} %broadcast_compare_fusion), kind=kLoop, calls=%fused_computation.14 | loop fusion | flops 8192 | bytes 8276 | tf_op jit(solution)/shard_map/jit(_where)/select_n | solution.py:264
  4.1 0.3 fusion.2
  4.5 0.8 pad_maximum_fusion
  5.2 0.7 compare_select_fusion.refs_9_
  5.9 0.0 collective-permute-done.refs_1_
  5.9 0.0 copy-start.3
  5.9 0.7 copy-done.3
  6.6 12.4 %shard_map.82 = (bf16[128,2560]{1,0:T(8,128)(2,1)}, f32[128,512]{1,0:T(8,128)}) custom-call(bf16[64,2560]{1,0:T(8,128)(2,1)} %refs_0_.1, bf16[64,2560]{1,0:T(8,128)(2,1)} %copy-done.3, bf16[64,512]{1,0:T(8,128)(2,1)} %refs_2_.1, bf16[64,512]{1,0:T(8,128)(2,1)} %refs_3_.1, bf16[2048,512]{1,0:T(8,128)(2,1)} %bitcast.30, bf16[2048,512]{1,0:T(8,128)(2,1)} %bitcast.31, ...), custom_call_target="tpu_custom_call" | custom-call | tf_op jit(solution)/shard_map/pallas_call | solution.py:279
  19.0 0.0 copy-start.2
  19.1 1.1 %copy.20 = f32[128,512]{0,1:T(8,128)S(1)} copy(f32[128,512]{1,0:T(8,128)} %get-tuple-element.8) | data formatting | bytes 524288 | tf_op jit(solution)/shard_map/reshape | solution.py:312
  20.2 1.0 %slice.30 = bf16[64,2560]{1,0:T(8,128)(2,1)S(1)} slice(bf16[128,2560]{1,0:T(8,128)(2,1)} %get-tuple-element.7), slice={[64:128], [0:2560]} | slice | bytes 655360 | tf_op jit(solution)/shard_map/slice | solution.py:313
  21.2 0.5 collective-permute-start.2
  21.7 0.1 fusion.6
  21.8 0.1 collective-permute-start.1
  21.9 1.1 %collective-permute-done.1 = f32[64,20]{0,1:T(8,128)S(1)} collective-permute-done((f32[64,20]{0,1:T(8,128)S(1)}, f32[64,20]{0,1:T(8,128)S(1)}, u32[]{:S(2)}, u32[]{:S(2)}) %collective-permute-start.1) | collective-permute-done | bytes 5152 | tf_op jit(solution)/shard_map/ppermute | solution.py:19
  23.0 0.1 copy.18
  23.1 0.1 copy.17
  23.2 0.0 copy-start.1
  23.2 0.0 collective-permute-done.2
  23.2 0.3 mul.67
  23.5 0.3 mul.70
  23.7 0.0 copy-done.2
  23.8 0.2 fusion.1.refs_0_
  24.0 0.6 copy-done.1
  24.6 56.6 %shard_map.83 = bf16[16,2,32,320]{3,2,1,0:T(8,128)(2,1)S(1)} custom-call(bf16[64,2560]{1,0:T(8,128)(2,1)S(1)} %fusion.1.refs_0_, bf16[320,2560]{1,0:T(8,128)(2,1)S(1)} %copy-done.1), custom_call_target="tpu_custom_call" | custom-call | tf_op jit(solution)/shard_map/pallas_call | solution.py:218
  81.2 0.5 copy.19
  81.7 1.5 %reshape.116 = bf16[64,5120]{1,0:T(8,128)(2,1)} reshape(bf16[64,16,320]{2,1,0:T(8,128)(2,1)S(1)} %copy.19) | data formatting | bytes 1310720 | tf_op jit(solution)/shard_map/reshape | solution.py:243
  (9 shorter events, 0.1 us)
Async XLA Ops:
  0.0 0.7 copy-start
  0.0 5.9 %collective-permute-start = (bf16[64,2560]{1,0:T(8,128)(2,1)}, bf16[64,2560]{1,0:T(8,128)(2,1)S(1)}, u32[]{:S(2)}, u32[]{:S(2)}) collective-permute-start(bf16[64,2560]{1,0:T(8,128)(2,1)} %refs_0_.1), channel_id=1, source_target_pairs={{0,2},{2,0},{4,6},{6,4},{8,10},{10,8},{12,14},{14,12},{16,18},{18,... | collective-permute-start | bytes 983048 | tf_op jit(solution)/shard_map/ppermute | solution.py:19
  5.9 0.7 copy-start.3
  19.0 4.7 %copy-start.2 = (bf16[128,2560]{1,0:T(8,128)(2,1)S(1)}, bf16[128,2560]{1,0:T(8,128)(2,1)}, u32[]{:S(2)}) copy-start(bf16[128,2560]{1,0:T(8,128)(2,1)} %get-tuple-element.7) | copy-start | bytes 1966084
  21.2 2.0 %collective-permute-start.2 = (bf16[64,2560]{1,0:T(8,128)(2,1)S(1)}, bf16[64,2560]{1,0:T(8,128)(2,1)S(1)}, u32[]{:S(2)}, u32[]{:S(2)}) collective-permute-start(bf16[64,2560]{1,0:T(8,128)(2,1)S(1)} %slice.30), channel_id=1, source_target_pairs={{0,2},{2,0},{4,6},{6,4},{8,10},{10,8},{12,14},{14,12},{16,18},{18,... | collective-permute-start | bytes 983048 | tf_op jit(solution)/shard_map/ppermute | solution.py:19
  21.8 1.2 %collective-permute-start.1 = (f32[64,20]{0,1:T(8,128)S(1)}, f32[64,20]{0,1:T(8,128)S(1)}, u32[]{:S(2)}, u32[]{:S(2)}) collective-permute-start(f32[64,20]{0,1:T(8,128)S(1)} %slice.27), channel_id=1, source_target_pairs={{0,2},{2,0},{4,6},{6,4},{8,10},{10,8},{12,14},{14,12},{16,18},{18,... | collective-permute-start | bytes 15368 | tf_op jit(solution)/shard_map/ppermute | solution.py:19
  23.2 1.4 %copy-start.1 = (bf16[320,2560]{1,0:T(8,128)(2,1)S(1)}, bf16[320,2560]{1,0:T(8,128)(2,1)}, u32[]{:S(2)}) copy-start(bf16[320,2560]{1,0:T(8,128)(2,1)} %refs_1_.1) | copy-start | bytes 4915204
